TPU v7x, 768 devices: a whole 4x8x12 slice. The times are simulated.
768 devices in a mesh: ctx: 24 (over z_lo, x), tp: 32 (over z_hi, y, core).
Axes of the slice: x: 4, y: 8, z: 12 (z_hi: 2, z_lo: 6; z = z_hi * 6 + z_lo), core: 2. Of those that a mesh axis runs over, the one named last changes fastest.
Arguments:
- grad_out: bfloat16 [3072, 5120], P('ctx', 'tp'), may hold values from -6 to 6
- w_out: bfloat16 [4096, 5120], P('tp'), may hold values from -0.078125 to 0.078125
- query_proj: bfloat16 [3072, 4096], P('ctx', 'tp'), may hold values from -6 to 6
- key_proj: bfloat16 [3072, 4096], P('ctx', 'tp'), may hold values from -6 to 6
- value_proj: bfloat16 [3072, 4096], P('ctx', 'tp'), may hold values from -6 to 6
- w_query: bfloat16 [5120, 4096], P(None, 'tp'), may hold values from -0.1875 to 0.1875
- w_key: bfloat16 [5120, 4096], P(None, 'tp'), may hold values from -0.09375 to 0.09375
- w_value: bfloat16 [5120, 4096], P(None, 'tp'), may hold values from -0.09375 to 0.09375
- tile_keys: int32 [24, 13], replicated, may hold values from 0 to 23, as said below
Outputs:
- input_grad: float32 [5120, 3072], P('tp', 'ctx')
Inputs may be any that keep to these rules, and one draw needn't show every extreme that they name: `tile_keys`: each row lists 13 distinct key tiles, among them the query tile itself; every listed tile u has |u - t| <= 12 for its query tile t.
All inputs are finite; a program needn't handle non-finite values.
Results may differ from a plain program's by a relative error of at most 0.0078.
Values may be sent and summed in bfloat16 or wider, within the bound.
A program may use at most 32 MiB of HBM per device.

v0:
```python
import jax
import jax.numpy as jnp
from jax import lax
from jax.sharding import PartitionSpec as P

TILE = 128


def on_device(
    grad_out, w_out, query_proj, key_proj, value_proj, w_query, w_key, w_value, tile_keys
):
    row_count = query_proj.shape[0]
    head_size = query_proj.shape[1]
    score_scale = head_size ** (-0.5)
    tiles_here = row_count // TILE
    slab_index = lax.axis_index("ctx")
    contract_last = (((1,), (1,)), ((), ()))
    contract_first = (((0,), (0,)), ((), ()))
    d_attn = lax.dot_general(
        lax.all_gather(grad_out, "tp", axis=1, tiled=True),
        w_out,
        contract_last,
        preferred_element_type=jnp.float32,
    ).astype(jnp.bfloat16)
    keys_all, values_all = (
        lax.all_gather(key_proj, "ctx", axis=0, tiled=True),
        lax.all_gather(value_proj, "ctx", axis=0, tiled=True),
    )
    total_tiles = keys_all.shape[0] // TILE
    own_lists = lax.dynamic_slice_in_dim(tile_keys, slab_index * tiles_here, tiles_here, 0)
    all_tiles = jnp.arange(total_tiles, dtype=jnp.int32)
    tile_ok = jnp.any(own_lists[:, :, None] == all_tiles[None, None, :], axis=1)
    token_mask = jnp.repeat(jnp.repeat(tile_ok, TILE, axis=0), TILE, axis=1)
    scores = (
        lax.dot_general(query_proj, keys_all, contract_last, preferred_element_type=jnp.float32)
        * score_scale
    )
    scores = jnp.where(token_mask, scores, -jnp.inf)
    row_max = jnp.max(scores, axis=1, keepdims=True)
    exponent = jnp.exp(scores - row_max)
    row_total = jnp.sum(exponent, axis=1, keepdims=True)
    prob_exact = exponent / row_total
    prob_half = prob_exact.astype(jnp.bfloat16)
    attn_out = jnp.dot(prob_half, values_all, preferred_element_type=jnp.float32)
    row_delta = jnp.sum(d_attn.astype(jnp.float32) * attn_out, axis=1, keepdims=True)
    d_prob = lax.dot_general(d_attn, values_all, contract_last, preferred_element_type=jnp.float32)
    d_score = (prob_exact * (d_prob - row_delta) * score_scale).astype(jnp.bfloat16)
    d_query = jnp.dot(d_score, keys_all, preferred_element_type=jnp.float32).astype(jnp.bfloat16)
    key_part = lax.dot_general(
        d_score, query_proj, contract_first, preferred_element_type=jnp.float32
    )
    value_part = lax.dot_general(
        prob_half, d_attn, contract_first, preferred_element_type=jnp.float32
    )
    key_sums = lax.psum_scatter(
        jnp.concatenate([key_part, value_part], axis=1), "ctx", scatter_dimension=0, tiled=True
    )
    d_key = key_sums[:, :head_size].astype(jnp.bfloat16)
    d_value = key_sums[:, head_size:].astype(jnp.bfloat16)
    feature_sum = lax.dot_general(
        w_query, d_query, contract_last, preferred_element_type=jnp.float32
    )
    feature_sum = feature_sum + lax.dot_general(
        w_key, d_key, contract_last, preferred_element_type=jnp.float32
    )
    feature_sum = feature_sum + lax.dot_general(
        w_value, d_value, contract_last, preferred_element_type=jnp.float32
    )
    return lax.psum_scatter(feature_sum, "tp", scatter_dimension=0, tiled=True)


def solution(mesh):
    return jax.shard_map(
        on_device,
        mesh=mesh,
        in_specs=(
            P("ctx", "tp"),
            P("tp", None),
            P("ctx", "tp"),
            P("ctx", "tp"),
            P("ctx", "tp"),
            P(None, "tp"),
            P(None, "tp"),
            P(None, "tp"),
            P(),
        ),
        out_specs=P("tp", "ctx"),
        check_vma=False,
    )
```

profile of v0, /device:TPU:1, one launch (start us, length us, event | category | flops | bytes accessed | tf_op | source)
XLA Modules:
  0.0 525.0 jit_solution(10905184365727740441)
XLA Ops:
  6.5 0.7 all-gather.2.cloned.1.call-update
  7.3 0.9 dynamic-slice_reduce_fusion
  8.2 0.1 fusion.14
  8.3 0.1 broadcast_bitcast_fusion
  8.4 81.6 %all_gather.9 = bf16[3072,128]{1,0:T(8,128)(2,1)S(1)} all-gather(bf16[128,128]{1,0:T(8,128)(2,1)} %param.12), channel_id=1, replica_groups=mesh['ctx'=24,'tp'=32] {'ctx'}, dimensions={0}, use_global_device_ids=true | all-gather | bytes 819200 | tf_op jit(solution)/shard_map/all_gather | solution.py:26
  90.0 1.2 fusion.17
  91.2 1.1 copy-done.1
  92.3 0.4 fusion.6
  92.7 71.7 %all_gather.11 = bf16[3072,128]{1,0:T(8,128)(2,1)} all-gather(bf16[128,128]{1,0:T(8,128)(2,1)S(1)} %copy-done.7), channel_id=1, replica_groups=mesh['ctx'=24,'tp'=32] {'ctx'}, dimensions={0}, use_global_device_ids=true | all-gather | bytes 819200 | tf_op jit(solution)/shard_map/all_gather | solution.py:27
  164.5 1.9 convolution_convert_fusion.1
  166.4 0.5 fusion.9
  166.9 0.6 copy-done.5
  167.5 0.6 fusion.7
  168.1 0.6 fusion.4
  168.8 0.1 copy-done.6
  168.9 0.4 fusion.18
  169.3 2.0 pad_maximum_fusion
  171.4 2.3 fusion.8
  173.7 170.5 %reduce-scatter.5.cloned.1.call-done = f32[128,256]{0,1:T(8,128)} async-done(((f32[3072,256]{0,1:T(8,128)}), f32[128,256]{0,1:T(8,128)}) %reduce-scatter.5.cloned.1.call-update) | async-done | bytes 131088 | tf_op jit(solution)/shard_map/reduce_scatter | solution.py:55
  344.3 0.9 convert.4
  345.2 2.8 convolution_add_fusion.1
  348.0 2.0 fusion
  350.0 3.3 copy.14
  353.3 165.2 %reduce-scatter.7.cloned.1.call-done = f32[160,128]{1,0:T(8,128)} async-done(((f32[5120,128]{1,0:T(8,128)}), f32[160,128]{1,0:T(8,128)}) %reduce-scatter.7.cloned.1.call-update) | async-done | bytes 81936 | tf_op jit(solution)/shard_map/reduce_scatter | solution.py:69
  (19 shorter events, 0.1 us)
Async XLA Ops:
  6.5 164.9 %copy-start = (bf16[5120,128]{1,0:T(8,128)(2,1)S(1)}, bf16[5120,128]{1,0:T(8,128)(2,1)}, u32[]{:S(2)}) copy-start(bf16[5120,128]{1,0:T(8,128)(2,1)} %param.14) | copy-start | bytes 3932164
  6.5 157.9 %all-gather.2.cloned.1.call-start = ((), (), s32[]{:S(2)}) async-start(), calls=%async_computation.2 | async-start | bytes 1351680 | tf_op jit(solution)/shard_map/all_gather | solution.py:20
  7.3 337.0 %reduce-scatter.5.cloned.1.call-start = ((), (), s32[]{:S(2)}) async-start(), calls=%async_computation.3 | async-start | bytes 3276800 | tf_op jit(solution)/shard_map/reduce_scatter | solution.py:55
  90.0 2.7 copy-start.7
  91.2 1.2 copy-start.1
  91.2 73.3 %copy-start.3 = (bf16[128,5120]{1,0:T(8,128)(2,1)S(1)}, bf16[128,5120]{1,0:T(8,128)(2,1)}, u32[]{:S(2)}) copy-start(bf16[128,5120]{1,0:T(8,128)(2,1)} %param.10) | copy-start | bytes 3932164
  164.5 1.9 copy-start.2
  166.4 1.1 copy-start.5
  168.1 0.8 copy-start.6
  171.3 347.2 %reduce-scatter.7.cloned.1.call-start = ((), (), s32[]{:S(2)}) async-start(), calls=%async_computation.4 | async-start | bytes 2703360 | tf_op jit(solution)/shard_map/reduce_scatter | solution.py:69
  345.2 2.8 copy-start.4
Sparse Core Ops, SparseCore 0:
  11.3 109.3 all-gather.1
  171.5 172.7 reduce-scatter.4
  353.4 165.0 reduce-scatter.6
where the time goes:
time: 529 us; the launch traced here: 525 us
  waiting for transfers between devices  336 us (64%)
  blocking collectives  153 us (29%)
  between operations  13.2 us (2%)
  matrix products  12.4 us (2%)
  local copies, waits for them, and re-layouts  6.13 us (1%)
    reduce_scatter x1, waiting for transfers between devices, on_device(): lax.psum_scatter(jnp.concatenate([key_part, value_part], axis=1), 'ctx',...  171 us
    reduce_scatter x1, waiting for transfers between devices, on_device(): return lax.psum_scatter(feature_sum, 'tp', scatter_dimension=0, tiled=True)  165 us
    all_gather x1, blocking collectives, on_device(): lax.all_gather(key_proj, 'ctx', axis=0, tiled=True)  81.6 us
    all_gather x1, blocking collectives, on_device(): lax.all_gather(value_proj, 'ctx', axis=0, tiled=True)  71.7 us
  transfers between devices with their start and end apart: 3, of which 2 were waited for; matrix products, arithmetic and copies ran while one was open for 1% of the time, Pallas kernels for 0%

commit v1 on v0

v1 whole, which is shorter than its diff:
```python
import functools

import jax
import jax.numpy as jnp
from jax import lax
from jax.experimental import pallas as pl
from jax.experimental.pallas import tpu as pltpu
from jax.sharding import PartitionSpec as P

TILE = 128
X = 4
Z = 6
Y = 8
SPAN = 3
WAYS = 2 * SPAN + 1
MASKED = -1e30
MESH = pl.DeviceIdType.MESH
BF16 = jnp.bfloat16
F32 = jnp.float32
RELAY = {0: ((6, 1), (6, 2), (2, -1)), 1: ((2, -1), (2, -2), (6, 1))}
NEAR = (1, -1, 2, -2)
AG_SENDS = {e: tuple((0, step) for step in NEAR) + RELAY[e] for e in (0, 1)}
PLACE = {4: 0, 3: 1, 5: 2, 2: 3, 6: 4, 1: 5, 7: 6, 0: 7}


def dot(a, b):
    return jnp.dot(a, b, preferred_element_type=F32)


def dot_last(a, b):
    return lax.dot_general(a, b, (((1,), (1,)), ((), ())), preferred_element_type=F32)


def way(i):
    return ((i + 1) // 2) * (1 - 2 * ((i + 1) % 2))


def kernel(
    g_hbm, wo_hbm, q_hbm, k_hbm, v_hbm, wq_hbm, wk_hbm, wv_hbm, lists, out_ref,
    g_all, wo, qbuf, kall, vall, kt, vt, wcat,
    probs, stat_local, o_send, o_stat_send, o_recv, o_stat_recv,
    o_sum, m_sum, l_sum, do_buf, do_stat, dk_sum, dv_sum, dq_send, dq_recv, dq_sum,
    dkv_send, dkv_recv, d_cat, sib_out, sib_in, f_own, sum_out, relay_in, end_in, z_out, z_in,
    load_sem, ag_ss, ag_rs, ag_sib_ss, ag_sib_rs, pair_send, pair_recv,
    kv_ss, kv_rs, q_ss, q_rs, o_ss, o_rs, do_ss, do_rs, dq_ss, dq_rs, dkv_ss, dkv_rs,
    sib_ss, sib_rs, sum_ss, relay_rs, end_rs,
):
    ctx, tp = lax.axis_index("ctx"), lax.axis_index("tp")
    z, x = ctx // X, ctx % X
    half, y, core = tp // (2 * Y), (tp // 2) % Y, tp % 2
    scale = TILE ** (-0.5)
    block = out_ref.shape[0]
    listed = lists.shape[0]

    def tp_of(h, row, c):
        return h * (2 * Y) + row * 2 + c

    def half_of(e):
        return half if e == 0 else 1 - half

    def rows_of(h, row, c):
        return pl.ds(pl.multiple_of(tp_of(h, row, c) * block, block), block)

    def tile_rows(a):
        return pl.ds(pl.multiple_of(a * TILE, TILE), TILE)

    sibling = (ctx, tp_of(half, y, 1 - core))
    pair = (ctx, tp_of(1 - half, y, core))

    def y_peer(step):
        return (ctx, tp_of(half, (y + step + Y) % Y, core))

    def x_peer(j):
        return (z * X + (x + j) % X, tp)

    def z_peer(d):
        return ((z + d) * X + x, tp)

    def z_valid(d):
        return jnp.logical_and(z + d >= 0, z + d < Z)

    def remote(src, dst, ss, rs, to):
        return pltpu.make_async_remote_copy(
            src_ref=src, dst_ref=dst, send_sem=ss, recv_sem=rs, device_id=to, device_id_type=MESH
        )

    loads = [
        pltpu.make_async_copy(src, dst, load_sem.at[n])
        for n, (src, dst) in enumerate((
            (g_hbm, g_all.at[rows_of(half, y, core)]),
            (k_hbm, kall.at[tile_rows(x)]),
            (v_hbm, vall.at[tile_rows(x)]),
            (q_hbm, qbuf.at[SPAN]),
            (wo_hbm, wo),
            (wq_hbm, wcat.at[:, 0:TILE]),
            (wk_hbm, wcat.at[:, TILE : 2 * TILE]),
            (wv_hbm, wcat.at[:, 2 * TILE : 3 * TILE]),
        ))
    ]
    for load in loads:
        load.start()

    barrier = pltpu.get_barrier_semaphore()
    for to in (sibling, pair, *map(y_peer, NEAR), x_peer(1), x_peer(2), x_peer(3)):
        pl.semaphore_signal(barrier, inc=1, device_id=to, device_id_type=MESH)
    expected = jnp.int32(9)
    for d in (1, -1, 2, -2, 3, -3):
        @pl.when(z_valid(d))
        def _():
            pl.semaphore_signal(barrier, inc=1, device_id=z_peer(d), device_id_type=MESH)

        expected = expected + jnp.where(z_valid(d), 1, 0)

    loads[0].wait()
    pl.semaphore_wait(barrier, expected)

    def ag_slot(e, rel):
        return g_all.at[rows_of(half_of(e), (y + rel) % Y, core)]

    def ag_send(e, n):
        rel, step = AG_SENDS[e][n]
        slot = ag_slot(e, rel)
        return remote(slot, slot, ag_ss.at[e, n], ag_rs.at[e, (rel - step) % Y], y_peer(step))

    def ag_sib(e, rel):
        slot = ag_slot(e, rel)
        return remote(slot, slot, ag_sib_ss.at[e, rel], ag_sib_rs.at[e, rel], sibling)

    def ag_sib_wait(e):
        for rel in (0, 1, 7, 2, 6, 3, 5, 4):
            slot = g_all.at[rows_of(half_of(e), (y + rel) % Y, 1 - core)]
            remote(slot, slot, ag_sib_ss.at[e, rel], ag_sib_rs.at[e, rel], sibling).wait_recv()

    def ag_own(e):
        for n in range(len(NEAR)):
            ag_send(e, n).start()
        ag_sib(e, 0).start()

    def ag_arrive(e, rels):
        for rel in rels:
            slot = ag_slot(e, rel)
            remote(slot, slot, ag_ss.at[e, 0], ag_rs.at[e, rel], y_peer(1)).wait_recv()
            for n, (source, _) in enumerate(AG_SENDS[e]):
                if source == rel:
                    ag_send(e, n).start()
            ag_sib(e, rel).start()

    own_slot = ag_slot(0, 0)
    other_slot = ag_slot(1, 0)
    pair_copy = remote(own_slot, own_slot, pair_send.at[0], pair_recv.at[0], pair)
    pair_copy.start()
    ag_own(0)
    for load in loads[1:4]:
        load.wait()

    def kv_copy(buf, which, j):
        slot = buf.at[tile_rows(x)]
        return remote(slot, slot, kv_ss.at[which, j], kv_rs.at[which, x], x_peer(j))

    for j in (1, 3, 2):
        kv_copy(kall, 0, j).start()
        kv_copy(vall, 1, j).start()

    def q_copy(d):
        return remote(qbuf.at[SPAN], qbuf.at[SPAN - d], q_ss.at[SPAN + d], q_rs.at[SPAN - d], z_peer(d))

    for d in (1, -1, 2, -2, 3, -3):
        @pl.when(z_valid(d))
        def _():
            q_copy(d).start()

    ag_arrive(0, (2, 6, 1, 7))

    for j in (1, 3, 2):
        source = (x + j) % X
        for which, buf in ((0, kall), (1, vall)):
            slot = buf.at[tile_rows(source)]
            remote(slot, slot, kv_ss.at[which, j], kv_rs.at[which, source], x_peer(j)).wait_recv()
    for a in range(X):
        part = slice(a * TILE, (a + 1) * TILE)
        kt[:, part] = kall[part, :].astype(F32).T.astype(BF16)
        vt[:, part] = vall[part, :].astype(F32).T.astype(BF16)

    row_index = lax.broadcasted_iota(jnp.int32, (8, TILE), 0)

    def o_copy(which, d):
        send, recv = ((o_send, o_recv), (o_stat_send, o_stat_recv))[which]
        return remote(
            send.at[SPAN + d], recv.at[SPAN - d], o_ss.at[which, SPAN + d], o_rs.at[which, SPAN - d], z_peer(d)
        )

    def scores_of(i, carry):
        d = way(i)

        @pl.when(z_valid(d))
        def _():
            @pl.when(d != 0)
            def _():
                q_copy(-d).wait_recv()

            tile = (z + d) * X + x
            s = dot_last(kall[...], qbuf[SPAN + d])
            parts = []
            for a in range(X):
                key_tile = z * X + a
                found = lists[0, tile] == key_tile
                for n in range(1, listed):
                    found = jnp.logical_or(found, lists[n, tile] == key_tile)
                bias = jnp.where(found, jnp.float32(0.0), jnp.float32(MASKED))
                parts.append(s[a * TILE : (a + 1) * TILE] * scale + bias)
            top = functools.reduce(jnp.maximum, parts)
            row_max = jnp.max(top, axis=0, keepdims=True)
            parts = [jnp.exp(part - row_max) for part in parts]
            row_total = jnp.sum(functools.reduce(jnp.add, parts), axis=0, keepdims=True)
            for a in range(X):
                probs[SPAN + d, a * TILE : (a + 1) * TILE, :] = parts[a]
            stat = jnp.where(row_index == 0, row_max, row_total)
            stat_local[SPAN + d] = stat
            o_part = dot(vt[...], jnp.concatenate([part.astype(BF16) for part in parts], axis=0))

            @pl.when(d == 0)
            def _():
                o_sum[...] = o_part
                m_sum[...] = row_max
                l_sum[...] = row_total

            @pl.when(d != 0)
            def _():
                o_send[SPAN + d] = o_part.astype(BF16)
                o_stat_send[SPAN + d] = stat
                o_copy(0, d).start()
                o_copy(1, d).start()

        return carry

    remote(other_slot, other_slot, pair_send.at[0], pair_recv.at[0], pair).wait_recv()
    ag_own(1)
    lax.fori_loop(0, 1, scores_of, 0)
    ag_arrive(0, (3, 5, 4))
    lax.fori_loop(1, 3, scores_of, 0)
    ag_arrive(1, (2, 6, 1, 7))
    lax.fori_loop(3, 7, scores_of, 0)
    ag_arrive(1, (3, 5, 4))

    def merge(i, carry):
        d = way(i)

        @pl.when(z_valid(d))
        def _():
            o_copy(0, -d).wait_recv()
            o_copy(1, -d).wait_recv()
            m_part = o_stat_recv[SPAN + d, 0:1, :]
            l_part = o_stat_recv[SPAN + d, 1:2, :]
            m_old = m_sum[...]
            m_new = jnp.maximum(m_old, m_part)
            w_old, w_part = jnp.exp(m_old - m_new), jnp.exp(m_part - m_new)
            m_sum[...] = m_new
            l_sum[...] = l_sum[...] * w_old + l_part * w_part
            o_sum[...] = o_sum[...] * w_old + o_recv[SPAN + d].astype(F32) * w_part

        return carry

    def d_attn_of(e):
        ag_sib_wait(e)
        span = Y * 2 * block
        part = pl.ds(pl.multiple_of(half_of(e) * span, TILE), span)
        return dot(wo[:, part], g_all[part, :])

    loads[4].wait()
    d_out = d_attn_of(0)
    lax.fori_loop(1, WAYS, merge, 0)
    d_out = (d_out + d_attn_of(1)).astype(BF16)
    do_buf[SPAN] = d_out
    inverse = 1.0 / l_sum[...]
    delta = jnp.sum(d_out.astype(F32) * o_sum[...], axis=0, keepdims=True) * inverse
    do_stat[SPAN] = jnp.where(row_index == 0, m_sum[...], jnp.where(row_index == 1, inverse, delta))

    def do_copy(which, d):
        buf = (do_buf, do_stat)[which]
        return remote(
            buf.at[SPAN], buf.at[SPAN - d], do_ss.at[which, SPAN + d], do_rs.at[which, SPAN - d], z_peer(d)
        )

    for d in (1, -1, 2, -2, 3, -3):
        @pl.when(z_valid(d))
        def _():
            do_copy(0, d).start()
            do_copy(1, d).start()

    def dq_copy(d):
        return remote(dq_send.at[SPAN + d], dq_recv.at[SPAN - d], dq_ss.at[SPAN + d], dq_rs.at[SPAN - d], z_peer(d))

    dk_sum[...] = jnp.zeros_like(dk_sum)
    dv_sum[...] = jnp.zeros_like(dv_sum)

    def gradients_of(i, carry):
        d = way(i)

        @pl.when(z_valid(d))
        def _():
            @pl.when(d != 0)
            def _():
                do_copy(0, -d).wait_recv()
                do_copy(1, -d).wait_recv()

            row_max = do_stat[SPAN + d, 0:1, :]
            inv = do_stat[SPAN + d, 1:2, :]
            row_delta = do_stat[SPAN + d, 2:3, :]
            weight = jnp.exp(stat_local[SPAN + d, 0:1, :] - row_max) * inv
            d_o = do_buf[SPAN + d]
            prob = probs[SPAN + d] * weight
            d_prob = dot(vall[...], d_o)
            d_score = (prob * (d_prob - row_delta) * scale).astype(BF16)
            dv_sum[...] += dot_last(prob.astype(BF16), d_o)
            dk_sum[...] += dot(d_score, qbuf[SPAN + d])
            d_q = dot(kt[...], d_score)

            @pl.when(d == 0)
            def _():
                dq_sum[...] = d_q

            @pl.when(d != 0)
            def _():
                dq_send[SPAN + d] = d_q.astype(BF16)
                dq_copy(d).start()

        return carry

    lax.fori_loop(0, WAYS, gradients_of, 0)

    def dkv_copy(j):
        return remote(dkv_send.at[j], dkv_recv.at[j], dkv_ss.at[j], dkv_rs.at[j], x_peer(j))

    for j in (1, 3, 2):
        tile = tile_rows((x + j) % X)
        dkv_send[j, 0:TILE, :] = dk_sum[tile, :].astype(BF16)
        dkv_send[j, TILE : 2 * TILE, :] = dv_sum[tile, :].astype(BF16)
        dkv_copy(j).start()

    def dq_add(i, carry):
        d = way(i)

        @pl.when(z_valid(d))
        def _():
            dq_copy(-d).wait_recv()
            dq_sum[...] += dq_recv[SPAN + d].astype(F32)

        return carry

    d_key = dk_sum[tile_rows(x), :]
    d_value = dv_sum[tile_rows(x), :]
    lax.fori_loop(1, WAYS, dq_add, 0)
    for j in (1, 3, 2):
        dkv_copy(j).wait_recv()
        d_key = d_key + dkv_recv[j, 0:TILE, :].astype(F32)
        d_value = d_value + dkv_recv[j, TILE : 2 * TILE, :].astype(F32)
    d_cat[0:TILE, :] = dq_sum[...].astype(BF16)
    d_cat[TILE : 2 * TILE, :] = d_key.T.astype(BF16)
    d_cat[2 * TILE : 3 * TILE, :] = d_value.T.astype(BF16)
    for load in loads[5:]:
        load.wait()

    def features(j, carry):
        rel = (4 + ((j + 1) // 2) * (1 - 2 * (j % 2))) % Y
        for e in (1, 0):
            start = pl.multiple_of(tp_of(half_of(e), (y + rel) % Y, 0) * block, block)
            both = dot(wcat[pl.ds(start, 2 * block), :], d_cat[...])
            first, second = both[:block], both[block:]
            f_own[j, e] = jnp.where(core == 0, first, second)
            sib_out[j, e] = jnp.where(core == 0, second, first).astype(BF16)
        sib_copy(j).start()
        return carry

    def sib_copy(j):
        return remote(sib_out.at[j], sib_in.at[j], sib_ss.at[j], sib_rs.at[j], sibling)

    def summed(e, rel):
        return f_own[PLACE[rel], e] + sib_in[PLACE[rel], e].astype(F32)

    def relay_wait(e, way_in):
        remote(
            sum_out.at[e, way_in], relay_in.at[e, way_in], sum_ss.at[e, way_in], relay_rs.at[e, way_in], y_peer(1)
        ).wait_recv()
        return relay_in[e, way_in].astype(F32)

    def sum_copy(e, n):
        step = ((-1, 1, (-2, 2)[e]) + (-2, 2, -1, 1))[n]
        dst, sem = (relay_in.at[e, n], relay_rs.at[e, n]) if n < 3 else (end_in.at[e, n - 3], end_rs.at[e, n - 3])
        return remote(sum_out.at[e, n], dst, sum_ss.at[e, n], sem, y_peer(step))

    def sum_send(e, n, value):
        sum_out[e, n] = value.astype(BF16)
        sum_copy(e, n).start()

    lax.fori_loop(0, 4, features, 0)
    for j in (0, 1, 2):
        sib_copy(j).wait_recv()
    for e in (1, 0):
        sum_send(e, 2, summed(e, 4))
        sum_send(e, 0, summed(e, 5))
        sum_send(e, 1, summed(e, 3))
    lax.fori_loop(4, 8, features, 0)
    for j in (3, 4, 5, 6, 7):
        sib_copy(j).wait_recv()
    for e in (1, 0):
        sum_send(e, 5, summed(e, 7))
        sum_send(e, 6, summed(e, 1))
    for e in (1, 0):
        for n, rel in ((3, 6), (4, 2)):
            value = summed(e, rel) + relay_wait(e, n - 3)
            if n - 3 == e:
                value = value + relay_wait(e, 2)
            sum_send(e, n, value)

    def sum_end(e):
        value = summed(e, 0)
        for n in (2, 3, 0, 1):
            remote(
                sum_out.at[e, n + 3], end_in.at[e, n], sum_ss.at[e, n + 3], end_rs.at[e, n], y_peer(1)
            ).wait_recv()
            value = value + end_in[e, n].astype(F32)
        return value

    z_out[...] = sum_end(1).astype(BF16)
    pair_sum = remote(z_out, z_in, pair_send.at[1], pair_recv.at[1], pair)
    pair_sum.start()
    out_ref[...] = sum_end(0)

    pair_copy.wait_send()
    for e in (0, 1):
        for n in range(7):
            ag_send(e, n).wait_send()
            sum_copy(e, n).wait_send()
        for rel in range(Y):
            ag_sib(e, rel).wait_send()
    for j in (1, 2, 3):
        kv_copy(kall, 0, j).wait_send()
        kv_copy(vall, 1, j).wait_send()
        dkv_copy(j).wait_send()

    def drain(i, carry):
        d = way(i)

        @pl.when(z_valid(d))
        def _():
            q_copy(d).wait_send()
            dq_copy(d).wait_send()
            for which in (0, 1):
                o_copy(which, d).wait_send()
                do_copy(which, d).wait_send()

        return carry

    lax.fori_loop(1, WAYS, drain, 0)

    def drain_sibling(i, carry):
        sib_copy(i).wait_send()
        return carry

    lax.fori_loop(0, Y, drain_sibling, 0)
    pair_sum.wait()
    out_ref[...] += z_in[...].astype(F32)


def on_device(
    grad_out, w_out, query_proj, key_proj, value_proj, w_query, w_key, w_value, tile_keys
):
    block = grad_out.shape[1]
    features = w_out.shape[1]
    dma = pltpu.SemaphoreType.DMA
    square = (TILE, TILE)
    column = (X * TILE, TILE)
    row = (1, TILE)
    stat = (WAYS, 8, TILE)
    piece = (block, TILE)
    anywhere = pl.BlockSpec(memory_space=pl.ANY)
    return pl.pallas_call(
        kernel,
        out_shape=jax.ShapeDtypeStruct(piece, F32),
        in_specs=[anywhere] * 8 + [pl.BlockSpec(memory_space=pltpu.SMEM)],
        out_specs=pl.BlockSpec(memory_space=pltpu.VMEM),
        scratch_shapes=[
            pltpu.VMEM((features, TILE), BF16),
            pltpu.VMEM(w_out.shape, BF16),
            pltpu.VMEM((WAYS, *square), BF16),
            pltpu.VMEM(column, BF16),
            pltpu.VMEM(column, BF16),
            pltpu.VMEM(column[::-1], BF16),
            pltpu.VMEM(column[::-1], BF16),
            pltpu.VMEM((features, 3 * TILE), BF16),
            pltpu.VMEM((WAYS, *column), F32),
            pltpu.VMEM(stat, F32),
            pltpu.VMEM((WAYS, *square), BF16),
            pltpu.VMEM(stat, F32),
            pltpu.VMEM((WAYS, *square), BF16),
            pltpu.VMEM(stat, F32),
            pltpu.VMEM(square, F32),
            pltpu.VMEM(row, F32),
            pltpu.VMEM(row, F32),
            pltpu.VMEM((WAYS, *square), BF16),
            pltpu.VMEM(stat, F32),
            pltpu.VMEM(column, F32),
            pltpu.VMEM(column, F32),
            pltpu.VMEM((WAYS, *square), BF16),
            pltpu.VMEM((WAYS, *square), BF16),
            pltpu.VMEM(square, F32),
            pltpu.VMEM((X, 2 * TILE, TILE), BF16),
            pltpu.VMEM((X, 2 * TILE, TILE), BF16),
            pltpu.VMEM((3 * TILE, TILE), BF16),
            pltpu.VMEM((Y, 2, *piece), BF16),
            pltpu.VMEM((Y, 2, *piece), BF16),
            pltpu.VMEM((Y, 2, *piece), F32),
            pltpu.VMEM((2, 7, *piece), BF16),
            pltpu.VMEM((2, 3, *piece), BF16),
            pltpu.VMEM((2, 4, *piece), BF16),
            pltpu.VMEM(piece, BF16),
            pltpu.VMEM(piece, BF16),
            dma((8,)),
            dma((2, 7)), dma((2, Y)),
            dma((2, Y)), dma((2, Y)),
            dma((2,)), dma((2,)),
            dma((2, X)), dma((2, X)),
            dma((WAYS,)), dma((WAYS,)),
            dma((2, WAYS)), dma((2, WAYS)),
            dma((2, WAYS)), dma((2, WAYS)),
            dma((WAYS,)), dma((WAYS,)),
            dma((X,)), dma((X,)),
            dma((Y,)), dma((Y,)),
            dma((2, 7)), dma((2, 3)), dma((2, 4)),
        ],
        compiler_params=pltpu.CompilerParams(
            collective_id=0, has_side_effects=True, vmem_limit_bytes=60 * 1024 * 1024
        ),
    )(grad_out.T, w_out, query_proj, key_proj, value_proj, w_query, w_key, w_value, tile_keys.T)


def solution(mesh):
    return jax.shard_map(
        on_device,
        mesh=mesh,
        in_specs=(
            P("ctx", "tp"),
            P("tp", None),
            P("ctx", "tp"),
            P("ctx", "tp"),
            P("ctx", "tp"),
            P(None, "tp"),
            P(None, "tp"),
            P(None, "tp"),
            P(),
        ),
        out_specs=P("tp", "ctx"),
        check_vma=False,
    )
```

time: 529 us -> 75 us (0.14)
  waiting for transfers between devices: 336 us -> 0 us
  blocking collectives: 153 us -> 0 us
  Pallas kernels: 0 us -> 73.2 us
  between operations: 13.2 us -> 0.01 us
  matrix products: 12.4 us -> 0 us
    reduce_scatter x2 -> x0, waiting for transfers between devices: 336 us -> none  [the longest x1 171 us: on_device(): lax.psum_scatter(jnp.concatenate([key_part, value_part], axis=1), 'ctx',...]
    all_gather x2 -> x0, blocking collectives: 153 us -> none  [the longest x1 81.6 us: on_device(): lax.all_gather(key_proj, 'ctx', axis=0, tiled=True)]
    pallas_call x0 -> x1, Pallas kernels: none -> 73.2 us  [on_device(): pl.pallas_call(kernel, out_shape=jax.ShapeDtypeStruct(piece, F32), in_spe...]
    dot_general x9 -> x0, matrix products: 12.4 us -> none  [the longest x1 2.77 us: on_device(): lax.dot_general(w_key, d_key, contract_last, preferred_element_type=jnp.f...]
  transfers between devices with their start and end apart: 3 -> 0, of which waited for: 2 -> 0; matrix products, arithmetic and copies ran while one was open for 1% -> 0% of each run, Pallas kernels for 0% -> 0%
where the time goes in v1:
time: 75 us; the launch traced here: 74.8 us
  Pallas kernels  73.2 us (98%)
  local copies, waits for them, and re-layouts  1.53 us (2%)
    pallas_call x1, Pallas kernels, on_device(): pl.pallas_call(kernel, out_shape=jax.ShapeDtypeStruct(piece, F32), in_spe...  73.2 us
    unnamed x1, local copies, waits for them, and re-layouts  1.53 us

profile of v1, /device:TPU:1, one launch (start us, length us, event | category | flops | bytes accessed | tf_op | source)
XLA Modules:
  0.0 74.8 jit_solution(16231465799642181723)
XLA Ops:
  0.0 73.2 %shard_map.91 = f32[160,128]{1,0:T(8,128)} custom-call(bf16[160,128]{1,0:T(8,128)(2,1)} %bitcast.2, bf16[128,5120]{1,0:T(8,128)(2,1)} %wo_hbm.1, bf16[128,128]{1,0:T(8,128)(2,1)} %q_hbm.1, bf16[128,128]{1,0:T(8,128)(2,1)} %k_hbm.1, bf16[128,128]{1,0:T(8,128)(2,1)} %v_hbm.1, bf16[5120,128]{1,0:T(8,128)(2,1)} %wq_hbm.1, bf16[5120,128]{1,0:T(8,128)(2,1)} %wk_hbm.1, ...), custom_call_target="tpu_custom_call" | custom-call | tf_op jit(solution)/shard_map/pallas_call | solution.py:477
  73.2 1.5 %copy.11 = f32[160,128]{1,0:T(8,128)} copy(f32[160,128]{1,0:T(8,128)} %shard_map.91) | data formatting | bytes 163840

commit v2 on v1

--- a/solution.py
+++ b/solution.py
@@ -17,9 +17,13 @@
 MESH = pl.DeviceIdType.MESH
 BF16 = jnp.bfloat16
 F32 = jnp.float32
-RELAY = {0: ((6, 1), (6, 2), (2, -1)), 1: ((2, -1), (2, -2), (6, 1))}
 NEAR = (1, -1, 2, -2)
-AG_SENDS = {e: tuple((0, step) for step in NEAR) + RELAY[e] for e in (0, 1)}
+AG_SENDS = {
+    0: tuple((0, step) for step in NEAR) + ((6, 1), (6, 2), (2, -1)),
+    1: tuple((0, step) for step in NEAR) + ((4, 1), (4, -1)),
+}
+SUM_STEPS = {0: (-1, 1, -2, -2, 2, -1, 1), 1: (1, -1, None, -2, 2, -1, 1)}
+SUM_SENDS = {e: tuple(n for n in range(7) if SUM_STEPS[e][n] is not None) for e in (0, 1)}
 PLACE = {4: 0, 3: 1, 5: 2, 2: 3, 6: 4, 1: 5, 7: 6, 0: 7}
 
 
@@ -33,6 +37,10 @@
 
 def way(i):
     return ((i + 1) // 2) * (1 - 2 * ((i + 1) % 2))
+
+
+def far_way(i):
+    return ((i + WAYS - 1) // WAYS) * (SPAN + 1 - (i + 1) // 2) * (1 - 2 * ((i + 1) % 2))
 
 
 def kernel(
@@ -41,7 +49,7 @@
     probs, stat_local, o_send, o_stat_send, o_recv, o_stat_recv,
     o_sum, m_sum, l_sum, do_buf, do_stat, dk_sum, dv_sum, dq_send, dq_recv, dq_sum,
     dkv_send, dkv_recv, d_cat, sib_out, sib_in, f_own, sum_out, relay_in, end_in, z_out, z_in,
-    load_sem, ag_ss, ag_rs, ag_sib_ss, ag_sib_rs, pair_send, pair_recv,
+    load_sem, ag_ss, ag_rs, ag_sib_ss, ag_sib_rs, pair_ss, pair_rs,
     kv_ss, kv_rs, q_ss, q_rs, o_ss, o_rs, do_ss, do_rs, dq_ss, dq_rs, dkv_ss, dkv_rs,
     sib_ss, sib_rs, sum_ss, relay_rs, end_rs,
 ):
@@ -65,7 +73,7 @@
         return pl.ds(pl.multiple_of(a * TILE, TILE), TILE)
 
     sibling = (ctx, tp_of(half, y, 1 - core))
-    pair = (ctx, tp_of(1 - half, y, core))
+    pairs = ((ctx, tp_of(1 - half, y, core)), (ctx, tp_of(1 - half, (y + Y // 2) % Y, core)))
 
     def y_peer(step):
         return (ctx, tp_of(half, (y + step + Y) % Y, core))
@@ -101,9 +109,9 @@
         load.start()
 
     barrier = pltpu.get_barrier_semaphore()
-    for to in (sibling, pair, *map(y_peer, NEAR), x_peer(1), x_peer(2), x_peer(3)):
+    for to in (sibling, *pairs, *map(y_peer, NEAR), x_peer(1), x_peer(2), x_peer(3)):
         pl.semaphore_signal(barrier, inc=1, device_id=to, device_id_type=MESH)
-    expected = jnp.int32(9)
+    expected = jnp.int32(10)
     for d in (1, -1, 2, -2, 3, -3):
         @pl.when(z_valid(d))
         def _():
@@ -145,13 +153,26 @@
                     ag_send(e, n).start()
             ag_sib(e, rel).start()
 
-    own_slot = ag_slot(0, 0)
-    other_slot = ag_slot(1, 0)
-    pair_copy = remote(own_slot, own_slot, pair_send.at[0], pair_recv.at[0], pair)
-    pair_copy.start()
-    ag_own(0)
+    def pair_copy(n):
+        slot = ag_slot(0, 0)
+        return remote(slot, slot, pair_ss.at[n], pair_rs.at[n], pairs[n])
+
+    def pair_wait(n):
+        slot = ag_slot(1, n * (Y // 2))
+        remote(slot, slot, pair_ss.at[n], pair_rs.at[n], pairs[n]).wait_recv()
+
+    pair_copy(0).start()
+    pair_copy(1).start()
     for load in loads[1:4]:
         load.wait()
+
+    def q_copy(d):
+        return remote(qbuf.at[SPAN], qbuf.at[SPAN - d], q_ss.at[SPAN + d], q_rs.at[SPAN - d], z_peer(d))
+
+    for d in (3, -3, 2, -2, 1, -1):
+        @pl.when(z_valid(d))
+        def _():
+            q_copy(d).start()
 
     def kv_copy(buf, which, j):
         slot = buf.at[tile_rows(x)]
@@ -161,13 +182,7 @@
         kv_copy(kall, 0, j).start()
         kv_copy(vall, 1, j).start()
 
-    def q_copy(d):
-        return remote(qbuf.at[SPAN], qbuf.at[SPAN - d], q_ss.at[SPAN + d], q_rs.at[SPAN - d], z_peer(d))
-
-    for d in (1, -1, 2, -2, 3, -3):
-        @pl.when(z_valid(d))
-        def _():
-            q_copy(d).start()
+    ag_own(0)
 
     ag_arrive(0, (2, 6, 1, 7))
 
@@ -190,7 +205,7 @@
         )
 
     def scores_of(i, carry):
-        d = way(i)
+        d = far_way(i)
 
         @pl.when(z_valid(d))
         def _():
@@ -233,14 +248,18 @@
 
         return carry
 
-    remote(other_slot, other_slot, pair_send.at[0], pair_recv.at[0], pair).wait_recv()
+    lax.fori_loop(0, 1, scores_of, 0)
+    pair_wait(0)
     ag_own(1)
-    lax.fori_loop(0, 1, scores_of, 0)
+    lax.fori_loop(1, 5, scores_of, 0)
+    pair_wait(1)
+    for n in (4, 5):
+        ag_send(1, n).start()
+    ag_sib(1, 4).start()
+    lax.fori_loop(5, 7, scores_of, 0)
     ag_arrive(0, (3, 5, 4))
-    lax.fori_loop(1, 3, scores_of, 0)
     ag_arrive(1, (2, 6, 1, 7))
-    lax.fori_loop(3, 7, scores_of, 0)
-    ag_arrive(1, (3, 5, 4))
+    ag_arrive(1, (3, 5))
 
     def merge(i, carry):
         d = way(i)
@@ -281,7 +300,7 @@
             buf.at[SPAN], buf.at[SPAN - d], do_ss.at[which, SPAN + d], do_rs.at[which, SPAN - d], z_peer(d)
         )
 
-    for d in (1, -1, 2, -2, 3, -3):
+    for d in (3, -3, 2, -2, 1, -1):
         @pl.when(z_valid(d))
         def _():
             do_copy(0, d).start()
@@ -294,7 +313,7 @@
     dv_sum[...] = jnp.zeros_like(dv_sum)
 
     def gradients_of(i, carry):
-        d = way(i)
+        d = far_way(i)
 
         @pl.when(z_valid(d))
         def _():
@@ -360,22 +379,22 @@
     for load in loads[5:]:
         load.wait()
 
-    def features(j, carry):
-        rel = (4 + ((j + 1) // 2) * (1 - 2 * (j % 2))) % Y
-        for e in (1, 0):
+    def features(e, m, carry):
+        for n, rel in enumerate((4 + m, 3 - m)):
             start = pl.multiple_of(tp_of(half_of(e), (y + rel) % Y, 0) * block, block)
             both = dot(wcat[pl.ds(start, 2 * block), :], d_cat[...])
             first, second = both[:block], both[block:]
-            f_own[j, e] = jnp.where(core == 0, first, second)
-            sib_out[j, e] = jnp.where(core == 0, second, first).astype(BF16)
-        sib_copy(j).start()
+            f_own[e, m, n] = jnp.where(core == 0, first, second)
+            sib_out[e, m, n] = jnp.where(core == 0, second, first).astype(BF16)
+        sib_copy(e, m).start()
         return carry
 
-    def sib_copy(j):
-        return remote(sib_out.at[j], sib_in.at[j], sib_ss.at[j], sib_rs.at[j], sibling)
+    def sib_copy(e, m):
+        return remote(sib_out.at[e, m], sib_in.at[e, m], sib_ss.at[e, m], sib_rs.at[e, m], sibling)
 
     def summed(e, rel):
-        return f_own[PLACE[rel], e] + sib_in[PLACE[rel], e].astype(F32)
+        m, n = PLACE[rel] // 2, PLACE[rel] % 2
+        return f_own[e, m, n] + sib_in[e, m, n].astype(F32)
 
     def relay_wait(e, way_in):
         remote(
@@ -384,33 +403,12 @@
         return relay_in[e, way_in].astype(F32)
 
     def sum_copy(e, n):
-        step = ((-1, 1, (-2, 2)[e]) + (-2, 2, -1, 1))[n]
         dst, sem = (relay_in.at[e, n], relay_rs.at[e, n]) if n < 3 else (end_in.at[e, n - 3], end_rs.at[e, n - 3])
-        return remote(sum_out.at[e, n], dst, sum_ss.at[e, n], sem, y_peer(step))
+        return remote(sum_out.at[e, n], dst, sum_ss.at[e, n], sem, y_peer(SUM_STEPS[e][n]))
 
     def sum_send(e, n, value):
         sum_out[e, n] = value.astype(BF16)
         sum_copy(e, n).start()
-
-    lax.fori_loop(0, 4, features, 0)
-    for j in (0, 1, 2):
-        sib_copy(j).wait_recv()
-    for e in (1, 0):
-        sum_send(e, 2, summed(e, 4))
-        sum_send(e, 0, summed(e, 5))
-        sum_send(e, 1, summed(e, 3))
-    lax.fori_loop(4, 8, features, 0)
-    for j in (3, 4, 5, 6, 7):
-        sib_copy(j).wait_recv()
-    for e in (1, 0):
-        sum_send(e, 5, summed(e, 7))
-        sum_send(e, 6, summed(e, 1))
-    for e in (1, 0):
-        for n, rel in ((3, 6), (4, 2)):
-            value = summed(e, rel) + relay_wait(e, n - 3)
-            if n - 3 == e:
-                value = value + relay_wait(e, 2)
-            sum_send(e, n, value)
 
     def sum_end(e):
         value = summed(e, 0)
@@ -421,15 +419,42 @@
             value = value + end_in[e, n].astype(F32)
         return value
 
-    z_out[...] = sum_end(1).astype(BF16)
-    pair_sum = remote(z_out, z_in, pair_send.at[1], pair_recv.at[1], pair)
-    pair_sum.start()
+    def pair_sum(n):
+        return remote(z_out.at[n], z_in.at[n], pair_ss.at[2 + n], pair_rs.at[2 + n], pairs[n])
+
+    half_places = Y // 2
+    lax.fori_loop(0, half_places, functools.partial(features, 1), 0)
+    lax.fori_loop(0, 2, functools.partial(features, 0), 0)
+    for m in range(half_places):
+        sib_copy(1, m).wait_recv()
+    for n, rel in ((0, 5), (1, 3), (3, 6), (4, 2), (5, 7), (6, 1)):
+        sum_send(1, n, summed(1, rel))
+    lax.fori_loop(2, half_places, functools.partial(features, 0), 0)
+    for m in (0, 1):
+        sib_copy(0, m).wait_recv()
+    for n, rel in ((2, 4), (0, 5), (1, 3)):
+        sum_send(0, n, summed(0, rel))
+    for m in (2, 3):
+        sib_copy(0, m).wait_recv()
+    for n, rel in ((5, 7), (6, 1)):
+        sum_send(0, n, summed(0, rel))
+    z_out[1] = (summed(1, 4) + relay_wait(1, 0) + relay_wait(1, 1)).astype(BF16)
+    pair_sum(1).start()
+    z_out[0] = sum_end(1).astype(BF16)
+    pair_sum(0).start()
+    for n, rel in ((3, 6), (4, 2)):
+        value = summed(0, rel) + relay_wait(0, n - 3)
+        if n == 3:
+            value = value + relay_wait(0, 2)
+        sum_send(0, n, value)
     out_ref[...] = sum_end(0)
 
-    pair_copy.wait_send()
+    for n in (0, 1):
+        pair_copy(n).wait_send()
     for e in (0, 1):
-        for n in range(7):
+        for n in range(len(AG_SENDS[e])):
             ag_send(e, n).wait_send()
+        for n in SUM_SENDS[e]:
             sum_copy(e, n).wait_send()
         for rel in range(Y):
             ag_sib(e, rel).wait_send()
@@ -453,13 +478,12 @@
 
     lax.fori_loop(1, WAYS, drain, 0)
 
-    def drain_sibling(i, carry):
-        sib_copy(i).wait_send()
-        return carry
-
-    lax.fori_loop(0, Y, drain_sibling, 0)
-    pair_sum.wait()
-    out_ref[...] += z_in[...].astype(F32)
+    for e in (0, 1):
+        for m in range(half_places):
+            sib_copy(e, m).wait_send()
+    pair_sum(0).wait()
+    pair_sum(1).wait()
+    out_ref[...] += z_in[0].astype(F32) + z_in[1].astype(F32)
 
 
 def on_device(
@@ -507,25 +531,25 @@
             pltpu.VMEM((X, 2 * TILE, TILE), BF16),
             pltpu.VMEM((X, 2 * TILE, TILE), BF16),
             pltpu.VMEM((3 * TILE, TILE), BF16),
-            pltpu.VMEM((Y, 2, *piece), BF16),
-            pltpu.VMEM((Y, 2, *piece), BF16),
-            pltpu.VMEM((Y, 2, *piece), F32),
+            pltpu.VMEM((2, Y // 2, 2, *piece), BF16),
+            pltpu.VMEM((2, Y // 2, 2, *piece), BF16),
+            pltpu.VMEM((2, Y // 2, 2, *piece), F32),
             pltpu.VMEM((2, 7, *piece), BF16),
             pltpu.VMEM((2, 3, *piece), BF16),
             pltpu.VMEM((2, 4, *piece), BF16),
-            pltpu.VMEM(piece, BF16),
-            pltpu.VMEM(piece, BF16),
+            pltpu.VMEM((2, *piece), BF16),
+            pltpu.VMEM((2, *piece), BF16),
             dma((8,)),
             dma((2, 7)), dma((2, Y)),
             dma((2, Y)), dma((2, Y)),
-            dma((2,)), dma((2,)),
+            dma((4,)), dma((4,)),
             dma((2, X)), dma((2, X)),
             dma((WAYS,)), dma((WAYS,)),
             dma((2, WAYS)), dma((2, WAYS)),
             dma((2, WAYS)), dma((2, WAYS)),
             dma((WAYS,)), dma((WAYS,)),
             dma((X,)), dma((X,)),
-            dma((Y,)), dma((Y,)),
+            dma((2, Y // 2)), dma((2, Y // 2)),
             dma((2, 7)), dma((2, 3)), dma((2, 4)),
         ],
         compiler_params=pltpu.CompilerParams(

time: 75 us -> 76.3 us (1.017)
  Pallas kernels: 73.2 us -> 74.6 us
    pallas_call x1, Pallas kernels: 73.2 us -> 74.6 us  [on_device(): pl.pallas_call(kernel, out_shape=jax.ShapeDtypeStruct(piece, F32), in_spe...]
where the time goes in v2:
time: 76.3 us; the launch traced here: 76.1 us
  Pallas kernels  74.6 us (98%)
  local copies, waits for them, and re-layouts  1.53 us (2%)
    pallas_call x1, Pallas kernels, on_device(): pl.pallas_call(kernel, out_shape=jax.ShapeDtypeStruct(piece, F32), in_spe...  74.6 us
    unnamed x1, local copies, waits for them, and re-layouts  1.53 us

profile of v2, /device:TPU:1, one launch (start us, length us, event | category | flops | bytes accessed | tf_op | source)
XLA Modules:
  0.0 76.1 jit_solution(3849692596356650061)
XLA Ops:
  0.0 74.6 %shard_map.91 = f32[160,128]{1,0:T(8,128)} custom-call(bf16[160,128]{1,0:T(8,128)(2,1)} %bitcast.2, bf16[128,5120]{1,0:T(8,128)(2,1)} %wo_hbm.1, bf16[128,128]{1,0:T(8,128)(2,1)} %q_hbm.1, bf16[128,128]{1,0:T(8,128)(2,1)} %k_hbm.1, bf16[128,128]{1,0:T(8,128)(2,1)} %v_hbm.1, bf16[5120,128]{1,0:T(8,128)(2,1)} %wq_hbm.1, bf16[5120,128]{1,0:T(8,128)(2,1)} %wk_hbm.1, ...), custom_call_target="tpu_custom_call" | custom-call | tf_op jit(solution)/shard_map/pallas_call | solution.py:501
  74.6 1.5 %copy.11 = f32[160,128]{1,0:T(8,128)} copy(f32[160,128]{1,0:T(8,128)} %shard_map.91) | data formatting | bytes 163840
